TPU v7x, 32 devices: a whole 2x2x4 slice. The times are simulated.
32 devices in a mesh: parts: 2 (over x), expert: 8 (over z, core), cuts: 2 (over y).
Axes of the slice: x: 2, y: 2, z: 4, core: 2. Of those that a mesh axis runs over, the one named last changes fastest.
Arguments:
- tokens: bfloat16 [128, 7168], P(('parts', 'expert', 'cuts')), parts along dimension 0, may hold values from -6 to 6
- route_ids: int32 [128, 8], P(('parts', 'expert', 'cuts')), parts along dimension 0, may hold values from 0 to 15, all different within a row; in each aligned block of 4 rows (0 to 3, 4 to 7, ...) at most 3 rows name the same one
- route_weight: float32 [128, 8], P(('parts', 'expert', 'cuts')), parts along dimension 0, may hold values from 0.05 to 0.5
- gate_weight: bfloat16 [16, 7168, 1024], P('expert', None, 'cuts'), may hold values from -0.0625 to 0.0625
- up_weight: bfloat16 [16, 7168, 1024], P('expert', None, 'cuts'), may hold values from -0.0625 to 0.0625
- down_weight: bfloat16 [16, 1024, 7168], P('expert', 'cuts'), may hold values from -0.1875 to 0.1875
Outputs:
- mixed: bfloat16 [128, 7168], P(('parts', 'expert', 'cuts')), parts along dimension 0
There are 2 independent parts, one for each index of `parts`. A program takes and returns all parts, laid end to end along the dimension named above; an argument that names none is the same for every part. Nothing has to cross between parts.
Inputs may be any that keep to these rules, and one draw needn't show every extreme that they name: `route_ids`: each row names 8 different experts. Among the rows of one device no expert is named more than 3 times, and in every draw some device's rows name some expert exactly 3 times.
All inputs are finite; a program needn't handle non-finite values. Where the computation divides by a largest or mean magnitude, that divisor is 1e-20 or more.
Results may differ from a plain program's by a relative error of at most 0.02.
Values may be sent and summed in bfloat16 or wider, within the bound.
A program may use at most 128 MiB of HBM per device.

v0:
```python
import math

import jax
import jax.numpy as jnp
from jax import lax
from jax.sharding import PartitionSpec as P

BLOCK = 128


eps = 1e-06
levels = 127.0


def hadamard(block_size):
    bit_count = block_size.bit_length() - 1
    row_bits = lax.broadcasted_iota(jnp.int32, (block_size, block_size), 0)
    col_bits = lax.broadcasted_iota(jnp.int32, (block_size, block_size), 1)
    shared_bits = jnp.bitwise_and(row_bits, col_bits)
    parity_sum = jnp.zeros((block_size, block_size), jnp.int32)
    for shift_step in range(bit_count):
        parity_sum = parity_sum + jnp.bitwise_and(jnp.right_shift(shared_bits, shift_step), 1)
    return (1 - 2 * (parity_sum % 2)).astype(jnp.bfloat16)


def expert_partial(quantized, scales, gate_weight, up_weight, down_weight):
    sources, experts, slot_count, feature_count = quantized.shape
    blocks = scales.shape[-1]
    restored = (
        quantized.astype(jnp.float32).reshape(
            sources, experts, slot_count, blocks, feature_count // blocks
        )
        * scales[..., None]
        / levels
    )
    restored = restored.reshape(sources, experts, slot_count, feature_count).astype(jnp.bfloat16)
    gate_value = jnp.einsum(
        "secd,edf->secf", restored, gate_weight, preferred_element_type=jnp.float32
    )
    upward = jnp.einsum("secd,edf->secf", restored, up_weight, preferred_element_type=jnp.float32)
    hidden = (jax.nn.silu(gate_value) * upward).astype(jnp.bfloat16)
    return jnp.einsum("secf,efd->secd", hidden, down_weight, preferred_element_type=jnp.float32)


def body(tokens, route_ids, route_weight, gate_weight, up_weight, down_weight):
    row_count, feature_count = tokens.shape
    top_count = route_ids.shape[1]
    local_experts = gate_weight.shape[0]
    expert_axis = lax.axis_size("expert")
    cut_axis = lax.axis_size("cuts")
    expert_total = local_experts * expert_axis
    capacity = min(row_count, row_count * top_count // expert_total + max(1, row_count // 8))
    blocks = feature_count // BLOCK
    sign_table = hadamard(BLOCK)
    rotated = jnp.dot(
        tokens.reshape(row_count * blocks, BLOCK), sign_table, preferred_element_type=jnp.float32
    ) * (1.0 / math.sqrt(BLOCK))
    largest = jnp.max(jnp.abs(rotated), axis=1) + eps
    quantized = (
        jnp.clip(jnp.floor(rotated / largest[:, None] * levels + 0.5), -levels, levels)
        .astype(jnp.bfloat16)
        .reshape(row_count, feature_count)
    )
    scales = largest.reshape(row_count, blocks)
    flat_ids = route_ids.reshape(-1)
    route_count = flat_ids.shape[0]
    expert_hot = (
        flat_ids[:, None] == lax.broadcasted_iota(jnp.int32, (route_count, expert_total), 1)
    ).astype(jnp.int32)
    earlier = jnp.cumsum(expert_hot, axis=0) - expert_hot
    position = jnp.sum(earlier * expert_hot, axis=1)
    slot_index = flat_ids * capacity + position
    slot_hot = (
        slot_index[:, None]
        == lax.broadcasted_iota(jnp.int32, (route_count, expert_total * capacity), 1)
    ).astype(jnp.float32)
    row_owner = lax.broadcasted_iota(jnp.int32, (route_count, row_count), 0) // top_count
    row_hot = (row_owner == lax.broadcasted_iota(jnp.int32, (route_count, row_count), 1)).astype(
        jnp.float32
    )
    placing = jnp.dot(slot_hot.T, row_hot, precision=lax.Precision.HIGHEST)
    combining = jnp.dot(
        (row_hot * route_weight.reshape(-1)[:, None]).T, slot_hot, precision=lax.Precision.HIGHEST
    )
    send_rows = jnp.dot(
        placing.astype(jnp.bfloat16), quantized, preferred_element_type=jnp.float32
    ).astype(jnp.bfloat16)
    send_rows = send_rows.reshape(expert_axis, local_experts, capacity, feature_count)
    send_scales = jnp.dot(placing, scales, precision=lax.Precision.HIGHEST).reshape(
        expert_axis, local_experts, capacity, blocks
    )
    peer_count = expert_axis * cut_axis
    wide_rows = jnp.broadcast_to(
        send_rows[:, None], (expert_axis, cut_axis) + send_rows.shape[1:]
    ).reshape((peer_count,) + send_rows.shape[1:])
    wide_scales = jnp.broadcast_to(
        send_scales[:, None], (expert_axis, cut_axis) + send_scales.shape[1:]
    ).reshape((peer_count,) + send_scales.shape[1:])
    partial_out = expert_partial(
        lax.all_to_all(wide_rows, ("expert", "cuts"), split_axis=0, concat_axis=0, tiled=True),
        lax.all_to_all(
            wide_scales.astype(jnp.bfloat16),
            ("expert", "cuts"),
            split_axis=0,
            concat_axis=0,
            tiled=True,
        ).astype(wide_scales.dtype),
        gate_weight,
        up_weight,
        down_weight,
    ).astype(jnp.bfloat16)
    returned = lax.all_to_all(
        partial_out, ("expert", "cuts"), split_axis=0, concat_axis=0, tiled=True
    )
    shaped = returned.reshape((expert_axis, cut_axis) + returned.shape[1:])
    outcome = jnp.sum(shaped.astype(jnp.float32), axis=1)
    outcome = outcome.reshape(expert_total * capacity, feature_count)
    mixed = jnp.dot(combining, outcome, precision=lax.Precision.HIGHEST)
    return mixed.astype(jnp.bfloat16)


def solution(mesh):
    in_specs = (
        P(("parts", "expert", "cuts"), None),
        P(("parts", "expert", "cuts"), None),
        P(("parts", "expert", "cuts"), None),
        P("expert", None, "cuts"),
        P("expert", None, "cuts"),
        P("expert", "cuts", None),
    )
    out_specs = P(("parts", "expert", "cuts"), None)
    return jax.shard_map(body, mesh=mesh, in_specs=in_specs, out_specs=out_specs, check_vma=False)
```

profile of v0, /device:TPU:11, one launch (start us, length us, event | category | flops | bytes accessed | tf_op | source)
XLA Modules:
  0.0 117.9 jit_solution(13901789188794877298)
XLA Ops:
  0.0 0.8 reshape.54
  0.8 0.1 fusion.39
  0.9 0.1 reduce_window_sum.11
  0.9 0.2 select_reduce_fusion
  1.1 0.3 fusion.37
  1.4 0.1 reshape.58
  1.5 0.1 copy.35
  1.6 0.9 reshape.55
  2.5 0.3 abs_reduce_fusion
  2.8 0.1 reshape.61
  2.9 0.2 convolution_convert_fusion.2
  3.2 0.7 reshape.66
  3.9 6.6 %all-to-all-start.1 = ((bf16[16,2,168]{2,1,0:T(2,128)(2,1)}), bf16[16,2,168]{2,1,0:T(2,128)(2,1)S(1)}, u32[]{:S(2)}, u32[]{:S(2)}) async-start(bf16[16,2,168]{2,1,0:T(2,128)(2,1)} %reshape.66), calls=%async_computation.1 | async-start | bytes 32768 | tf_op jit(solution)/shard_map/all_to_all | solution.py:101
  10.5 0.1 fusion.28
  10.6 0.4 convolution_convert_fusion
  11.0 0.4 broadcast_in_dim.6
  11.5 0.6 copy.33
  12.1 3.5 %all-to-all-done.1 = bf16[16,2,168]{2,1,0:T(2,128)(2,1)S(1)} async-done(((bf16[16,2,168]{2,1,0:T(2,128)(2,1)}), bf16[16,2,168]{2,1,0:T(2,128)(2,1)S(1)}, u32[]{:S(2)}, u32[]{:S(2)}) %all-to-all-start.1) | async-done | bytes 10784 | tf_op jit(solution)/shard_map/all_to_all | solution.py:101
  15.5 1.8 %broadcast_in_dim.7 = bf16[8,2,2,3,7168]{4,2,3,1,0:T(2,128)(2,1)} broadcast(bf16[8,2,3,7168]{3,1,2,0:T(2,128)(2,1)S(1)} %copy.33), dimensions={0,2,3,4} | broadcast | bytes 2064384 | tf_op jit(solution)/shard_map/broadcast_in_dim | solution.py:93
  17.3 5.6 %all-to-all-start = ((bf16[16,2,3,7168]{3,1,2,0:T(2,128)(2,1)}), bf16[16,2,3,7168]{3,1,2,0:T(2,128)(2,1)}, u32[]{:S(2)}, u32[]{:S(2)}) async-start(bf16[16,2,3,7168]{3,1,2,0:T(2,128)(2,1)} %bitcast.1), calls=%async_computation | async-start | bytes 2752512 | tf_op jit(solution)/shard_map/all_to_all | solution.py:100
  22.9 0.1 reshape.67
  23.1 2.0 %mul.63 = f32[16,2,3,56,128]{4,3,0,2,1:T(8,128)} broadcast(f32[16,2,3,56]{3,0,2,1:T(8,128)S(1)} %copy_convert_fusion), dimensions={0,1,2,3} | broadcast | bytes 2774016 | tf_op jit(solution)/shard_map/mul | solution.py:30
  25.0 2.6 %mul.64 = f32[16,2,3,7168]{3,0,2,1:T(8,128)S(1)} reshape(f32[16,2,3,56,128]{4,3,0,2,1:T(8,128)} %mul.63) | data formatting | bytes 5505024 | tf_op jit(solution)/shard_map/mul | solution.py:30
  27.6 28.2 %all-to-all-done = bf16[16,2,3,7168]{3,1,2,0:T(2,128)(2,1)} async-done(((bf16[16,2,3,7168]{3,1,2,0:T(2,128)(2,1)}), bf16[16,2,3,7168]{3,1,2,0:T(2,128)(2,1)}, u32[]{:S(2)}, u32[]{:S(2)}) %all-to-all-start) | async-done | bytes 1376288 | tf_op jit(solution)/shard_map/all_to_all | solution.py:100
  55.8 0.0 slice-start
  55.8 0.0 slice-start.1
  55.8 7.8 %fusion.12 = f32[16,2,3,512]{3,0,2,1:T(8,128)S(1)} fusion(bf16[2,7168,512]{2,1,0:T(8,128)(2,1)} %param.9, f32[16,2,3,7168]{3,0,2,1:T(8,128)S(1)} %mul.64, bf16[16,2,3,7168]{3,1,2,0:T(2,128)(2,1)} %all-to-all-done), kind=kOutput, calls=%fused_computation.12 | convolution fusion | flops 707395584 | bytes 19005440 | tf_op jit(solution)/shard_map/secd,edf->secf/dot_general | solution.py:37
  63.6 0.0 slice-start.2
  63.6 0.0 slice-start.3
  63.6 7.8 %fusion.21 = bf16[16,2,3,512]{3,0,2,1:T(8,128)(2,1)S(1)} fusion(bf16[2,7168,512]{2,1,0:T(8,128)(2,1)} %param.10, f32[16,2,3,512]{3,0,2,1:T(8,128)S(1)} %fusion.12, f32[16,2,3,7168]{3,0,2,1:T(8,128)S(1)} %mul.64, bf16[16,2,3,7168]{3,1,2,0:T(2,128)(2,1)} %all-to-all-done), kind=kOutput, calls=%fused_computation.15 | convolution fusion | flops 707690496 | bytes 19103744 | tf_op jit(solution)/shard_map/secd,edf->secf/dot_general | solution.py:40
  71.5 0.0 slice-done
  71.5 0.0 slice-done.1
  71.5 0.0 slice-done.2
  71.5 0.0 slice-done.3
  71.5 2.7 %fusion.9 = bf16[16,2,3,7168]{3,0,2,1:T(8,128)(2,1)S(1)} fusion(bf16[16,2,3,512]{3,0,2,1:T(8,128)(2,1)S(1)} %fusion.21, bf16[2,512,7168]{2,1,0:T(8,128)(2,1)S(1)} %bitcast.62), kind=kOutput, calls=%fused_computation.7 | convolution fusion | flops 705331200 | bytes 16154624 | tf_op jit(solution)/shard_map/secf,efd->secd/dot_general | solution.py:42
  74.2 0.0 copy-start
  74.2 2.5 %copy.38 = bf16[16,2,3,7168]{3,1,2,0:T(2,128)(2,1)} copy(bf16[16,2,3,7168]{3,0,2,1:T(8,128)(2,1)S(1)} %fusion.9) | data formatting | bytes 2752512 | tf_op jit(solution)/shard_map/convert_element_type | solution.py:111
  76.7 3.9 %all-to-all-start.2 = ((bf16[16,2,3,7168]{3,1,2,0:T(2,128)(2,1)}), bf16[16,2,3,7168]{3,1,2,0:T(2,128)(2,1)S(1)}, u32[]{:S(2)}, u32[]{:S(2)}) async-start(bf16[16,2,3,7168]{3,1,2,0:T(2,128)(2,1)} %copy.38), calls=%async_computation.2 | async-start | bytes 2752512 | tf_op jit(solution)/shard_map/all_to_all | solution.py:112
  80.6 0.0 copy-done
  80.6 0.1 mul.54
  80.7 0.3 fusion.38
  81.0 32.4 %all-to-all-done.2 = bf16[16,2,3,7168]{3,1,2,0:T(2,128)(2,1)S(1)} async-done(((bf16[16,2,3,7168]{3,1,2,0:T(2,128)(2,1)}), bf16[16,2,3,7168]{3,1,2,0:T(2,128)(2,1)S(1)}, u32[]{:S(2)}, u32[]{:S(2)}) %all-to-all-start.2) | async-done | bytes 1376288 | tf_op jit(solution)/shard_map/all_to_all | solution.py:112
  113.4 1.6 %convert_reduce_fusion = f32[8,2,3,7168]{3,1,2,0:T(2,128)S(1)} fusion(bf16[16,2,3,7168]{3,1,2,0:T(2,128)(2,1)S(1)} %all-to-all-done.2), kind=kLoop, calls=%fused_computation.10 | loop fusion | flops 1032192 | bytes 2752512 | tf_op jit(solution)/shard_map/reduce_sum | solution.py:116
  115.0 0.7 copy.40
  115.7 0.7 reshape.59
  116.5 1.4 %convolution_convert_fusion.1 = bf16[4,7168]{1,0:T(4,128)(2,1)} fusion(f32[4,48]{1,0:T(4,128)S(1)} %fusion.38, f32[48,7168]{1,0:T(8,128)S(1)} %reshape.59), kind=kOutput, calls=%fused_computation.9 | convolution fusion | flops 16543744 | bytes 1434368 | tf_op jit(solution)/shard_map/dot_general | solution.py:118
  (9 shorter events, 0.1 us)
Async XLA Ops:
  3.9 11.7 %all-to-all-start.1 = ((bf16[16,2,168]{2,1,0:T(2,128)(2,1)}), bf16[16,2,168]{2,1,0:T(2,128)(2,1)S(1)}, u32[]{:S(2)}, u32[]{:S(2)}) async-start(bf16[16,2,168]{2,1,0:T(2,128)(2,1)} %reshape.66), calls=%async_computation.1 | async-start | bytes 32768 | tf_op jit(solution)/shard_map/all_to_all | solution.py:101
  17.3 38.5 %all-to-all-start = ((bf16[16,2,3,7168]{3,1,2,0:T(2,128)(2,1)}), bf16[16,2,3,7168]{3,1,2,0:T(2,128)(2,1)}, u32[]{:S(2)}, u32[]{:S(2)}) async-start(bf16[16,2,3,7168]{3,1,2,0:T(2,128)(2,1)} %bitcast.1), calls=%async_computation | async-start | bytes 2752512 | tf_op jit(solution)/shard_map/all_to_all | solution.py:100
  55.8 15.6 %slice-start = ((s8[14680064]{0:T(1024)(128)(4,1)}), s8[4194304]{0:T(1024)(128)(4,1)S(1)}, s32[]{:S(2)}) async-start(s8[14680064]{0:T(1024)(128)(4,1)} %bitcast.61), calls=%async_computation.3 | async-start | bytes 8388608
  55.8 15.6 %slice-start.1 = ((s8[14680064]{0:T(1024)(128)(4,1)}), s8[4194304]{0:T(1024)(128)(4,1)S(1)}, s32[]{:S(2)}) async-start(s8[14680064]{0:T(1024)(128)(4,1)} %bitcast.61), calls=%async_computation.4 | async-start | bytes 8388608
  63.6 7.9 %slice-start.2 = ((s8[14680064]{0:T(1024)(128)(4,1)}), s8[4194304]{0:T(1024)(128)(4,1)S(1)}, s32[]{:S(2)}) async-start(s8[14680064]{0:T(1024)(128)(4,1)} %bitcast.61), calls=%async_computation.5 | async-start | bytes 8388608
  63.6 7.9 %slice-start.3 = ((s8[14680064]{0:T(1024)(128)(4,1)}), s8[2097152]{0:T(1024)(128)(4,1)S(1)}, s32[]{:S(2)}) async-start(s8[14680064]{0:T(1024)(128)(4,1)} %bitcast.61), calls=%async_computation.6 | async-start | bytes 4194304
  74.2 6.5 %copy-start = (f32[4,8]{1,0:T(4,128)S(1)}, f32[4,8]{1,0:T(4,128)}, u32[]{:S(2)}) copy-start(f32[4,8]{1,0:T(4,128)} %param.8) | copy-start | bytes 388
  76.7 36.7 %all-to-all-start.2 = ((bf16[16,2,3,7168]{3,1,2,0:T(2,128)(2,1)}), bf16[16,2,3,7168]{3,1,2,0:T(2,128)(2,1)S(1)}, u32[]{:S(2)}, u32[]{:S(2)}) async-start(bf16[16,2,3,7168]{3,1,2,0:T(2,128)(2,1)} %copy.38), calls=%async_computation.2 | async-start | bytes 2752512 | tf_op jit(solution)/shard_map/all_to_all | solution.py:112
where the time goes:
time: 118 us
  waiting for transfers between devices  64.1 us (54%)
  matrix products  21.1 us (18%)
  starting transfers between devices  16.2 us (14%)
  local copies, waits for them, and re-layouts  14.3 us (12%)
  other arithmetic  2.05 us (2%)
    all_to_all x1, waiting for transfers between devices, body(): lax.all_to_all(partial_out, ('expert', 'cuts'), split_axis=0, concat_axis...  32.4 us
    all_to_all x1, waiting for transfers between devices, body(): lax.all_to_all(wide_rows, ('expert', 'cuts'), split_axis=0, concat_axis=0...  28.2 us
    dot_general x1, matrix products, expert_partial(): jnp.einsum('secd,edf->secf', restored, up_weight, preferred_element_type=...  7.8 us
    dot_general x1, matrix products, expert_partial(): jnp.einsum('secd,edf->secf', restored, gate_weight, preferred_element_typ...  7.77 us
    all_to_all x1, starting transfers between devices, body(): lax.all_to_all(wide_scales.astype(jnp.bfloat16), ('expert', 'cuts'), spli...  6.61 us
    all_to_all x1, starting transfers between devices, body(): lax.all_to_all(wide_rows, ('expert', 'cuts'), split_axis=0, concat_axis=0...  5.61 us
    mul x2, local copies, waits for them, and re-layouts, expert_partial(): quantized.astype(jnp.float32)  4.58 us
    all_to_all x1, starting transfers between devices, body(): lax.all_to_all(partial_out, ('expert', 'cuts'), split_axis=0, concat_axis...  3.94 us
  transfers between devices with their start and end apart: 3, of which 3 were waited for; matrix products, arithmetic and copies ran while one was open for 6% of the time, Pallas kernels for 0%

commit v1 on v0

v1 whole, which is shorter than its diff:
```python
import functools
import math

import jax
import jax.numpy as jnp
from jax import lax
from jax.experimental import pallas as pl
from jax.experimental.pallas import tpu as pltpu
from jax.sharding import PartitionSpec as P

BLOCK = 128
eps = 1e-06
levels = 127.0
CORES = 2
QUARTERS = 4
TILE = 16
GROUP = 16
CHUNKS = 2
MESH = pl.DeviceIdType.MESH


def hadamard():
    row_bits = lax.broadcasted_iota(jnp.int32, (BLOCK, BLOCK), 0)
    col_bits = lax.broadcasted_iota(jnp.int32, (BLOCK, BLOCK), 1)
    shared = jnp.bitwise_and(row_bits, col_bits)
    for shift in (4, 2, 1):
        shared = jnp.bitwise_xor(shared, jnp.right_shift(shared, shift))
    return (1 - 2 * jnp.bitwise_and(shared, 1)).astype(jnp.float32).astype(jnp.bfloat16)


def permutation(rows, transposed):
    side = GROUP * TILE
    a = lax.broadcasted_iota(jnp.int32, (side, side), 1 if transposed else 0)
    b = lax.broadcasted_iota(jnp.int32, (side, side), 0 if transposed else 1)
    per = GROUP * rows
    quarter, inner = a // per, a % per
    source = (inner // rows) * TILE + quarter * rows + inner % rows
    return jnp.where(source == b, 1.0, 0.0).astype(jnp.bfloat16)


def kernel(
    n_z,
    n_y,
    tokens,
    ids,
    weights,
    gate_hbm,
    up_hbm,
    down_hbm,
    out,
    gate,
    up,
    down,
    gathered,
    stage,
    acc,
    hid,
    wide,
    y_buf,
    r_core,
    s_buf,
    r_y,
    t_buf,
    r_z,
    final,
    g_sem,
    u_sem,
    d_sem,
    az_send,
    az_recv,
    ay_send,
    ay_recv,
    ac_send,
    ac_recv,
    rc_send,
    rc_recv,
    ry_send,
    ry_recv,
    rz_send,
    rz_recv,
):
    rows, features = tokens.shape
    experts = gate.shape[0]
    units = gate.shape[2]
    width = features // QUARTERS
    chunk = width // CHUNKS
    plane = n_y * n_z
    blocks = CORES * plane
    groups = blocks // GROUP
    expert = lax.axis_index("expert")
    y = lax.axis_index("cuts")
    z, c = expert // CORES, expert % CORES
    far = 1 - c

    def peer(z_at, c_at, y_at):
        return {"expert": z_at * CORES + c_at, "cuts": y_at}

    def block(c_at, y_at, z_at):
        return (c_at * n_y + y_at) * n_z + z_at

    def z_next(step):
        return lax.rem(z + step, n_z)

    def y_next(step):
        return lax.rem(y + step, n_y)

    def z_prev(step):
        return lax.rem(z + n_z - step, n_z)

    def y_prev(step):
        return lax.rem(y + n_y - step, n_y)

    gate_in, up_in, down_in = [], [], []
    for q in range(QUARTERS):
        span = pl.ds(q * width, width)
        gate_in.append(
            pltpu.make_async_copy(gate_hbm.at[:, span, :], gate.at[:, span, :], g_sem.at[q])
        )
        up_in.append(pltpu.make_async_copy(up_hbm.at[:, span, :], up.at[:, span, :], u_sem.at[q]))
        gate_in[q].start()
        up_in[q].start()
    for j in range(CHUNKS):
        for q in range(QUARTERS):
            span = pl.ds(q * width + j * chunk, chunk)
            down_in.append(
                pltpu.make_async_copy(
                    down_hbm.at[:, :, span], down.at[:, :, span], d_sem.at[j * QUARTERS + q]
                )
            )
            down_in[-1].start()

    barrier = pltpu.get_barrier_semaphore()
    for step in range(1, n_z):
        pl.semaphore_signal(
            barrier, inc=1, device_id=peer(z_next(step), c, y), device_id_type=MESH
        )
    for step in range(1, n_y):
        pl.semaphore_signal(
            barrier, inc=1, device_id=peer(z, c, y_next(step)), device_id_type=MESH
        )
    pl.semaphore_signal(barrier, inc=1, device_id=peer(z, far, y), device_id_type=MESH)

    mine = block(c, y, z)
    for q in range(QUARTERS):
        stage[q * rows : (q + 1) * rows, :width] = tokens[:, q * width : (q + 1) * width].astype(
            jnp.float32
        )
    pieces = width // BLOCK
    stacked = jnp.concatenate(
        [stage[:, b * BLOCK : (b + 1) * BLOCK].astype(jnp.bfloat16) for b in range(pieces)], axis=0
    )
    rotated = jnp.dot(stacked, hadamard(), preferred_element_type=jnp.float32) * (
        1.0 / math.sqrt(BLOCK)
    )
    largest = jnp.max(jnp.abs(rotated), axis=1, keepdims=True) + eps
    quantized = jnp.clip(jnp.floor(rotated / largest * levels + 0.5), -levels, levels)
    restored = (quantized * largest / levels).astype(jnp.bfloat16)
    for b in range(pieces):
        gathered[mine, :, b * BLOCK : (b + 1) * BLOCK] = restored[b * TILE : (b + 1) * TILE, :]
    lane = lax.broadcasted_iota(jnp.int32, (rows, BLOCK), 1)
    dense = jnp.zeros((rows, BLOCK), jnp.float32)
    for k in range(ids.shape[1]):
        dense = dense + jnp.where(ids[:, k : k + 1] == lane, weights[:, k : k + 1], 0.0)
    stage[:, width:] = jnp.zeros((TILE, BLOCK), jnp.float32)
    for q in range(3):
        term = dense.astype(jnp.bfloat16).astype(jnp.float32)
        stage[q * rows : (q + 1) * rows, width:] = term
        dense = dense - term
    gathered[mine, :, width:] = stage[:, width:].astype(jnp.bfloat16)

    pl.semaphore_wait(barrier, n_z + n_y - 1)

    sent = []

    def push(src, dst, send_sem, recv_sem, device):
        copy = pltpu.make_async_remote_copy(
            src_ref=src,
            dst_ref=dst,
            send_sem=send_sem,
            recv_sem=recv_sem,
            device_id=device,
            device_id_type=MESH,
        )
        copy.start()
        sent.append(copy)

    def arrived(dst, send_sem, recv_sem, device):
        pltpu.make_async_remote_copy(
            src_ref=dst,
            dst_ref=dst,
            send_sem=send_sem,
            recv_sem=recv_sem,
            device_id=device,
            device_id_type=MESH,
        ).wait_recv()

    def to_y(z_step, slot):
        for step in range(1, n_y):
            push(
                gathered.at[slot],
                gathered.at[slot],
                ay_send.at[step, z_step],
                ay_recv.at[step, z_step],
                peer(z, c, y_next(step)),
            )

    def to_core(y_step, z_step, slot):
        push(
            gathered.at[slot],
            gathered.at[slot],
            ac_send.at[y_step, z_step],
            ac_recv.at[y_step, z_step],
            peer(z, far, y),
        )

    for step in range(n_z - 1, 0, -1):
        push(
            gathered.at[mine],
            gathered.at[mine],
            az_send.at[step],
            az_recv.at[step],
            peer(z_next(step), c, y),
        )
    to_y(0, mine)
    to_core(0, 0, mine)
    for z_step in range(1, n_z):
        slot = block(c, y, z_prev(z_step))
        arrived(
            gathered.at[slot], az_send.at[z_step], az_recv.at[z_step], peer(z_next(z_step), c, y)
        )
        to_y(z_step, slot)
        to_core(0, z_step, slot)
    for z_step in range(n_z):
        for y_step in range(1, n_y):
            slot = block(c, y_prev(y_step), z_prev(z_step))
            arrived(
                gathered.at[slot],
                ay_send.at[y_step, z_step],
                ay_recv.at[y_step, z_step],
                peer(z, c, y_next(y_step)),
            )
            to_core(y_step, z_step, slot)
    for z_step in range(n_z):
        for y_step in range(n_y):
            slot = block(far, y_prev(y_step), z_prev(z_step))
            arrived(
                gathered.at[slot],
                ac_send.at[y_step, z_step],
                ac_recv.at[y_step, z_step],
                peer(z, far, y),
            )

    order = permutation(rows, False)
    per = GROUP * rows
    route = []
    for g in range(groups):
        flat = gathered[g * GROUP : (g + 1) * GROUP].reshape(GROUP * TILE, width + BLOCK)
        ordered = jnp.dot(order, flat, preferred_element_type=jnp.float32)
        wide[g] = ordered[:, :width].astype(jnp.bfloat16)
        terms = ordered[:, width:]
        route.append(terms[:per] + terms[per : 2 * per] + terms[2 * per : 3 * per])
    for q in range(QUARTERS):
        span = slice(q * width, (q + 1) * width)
        gate_in[q].wait()
        for g in range(groups):
            x = wide[g, q * per : (q + 1) * per, :]
            for e in range(experts):
                part = jnp.dot(x, gate[e, span, :], preferred_element_type=jnp.float32)
                acc[g, 0, e] = part if q == 0 else acc[g, 0, e] + part
        up_in[q].wait()
        for g in range(groups):
            x = wide[g, q * per : (q + 1) * per, :]
            for e in range(experts):
                part = jnp.dot(x, up[e, span, :], preferred_element_type=jnp.float32)
                acc[g, 1, e] = part if q == 0 else acc[g, 1, e] + part
    lanes = lax.broadcasted_iota(jnp.int32, (per, BLOCK), 1)
    scale = []
    for g in range(groups):
        for e in range(experts):
            v = acc[g, 0, e]
            hid[g, e] = (v / (1.0 + jnp.exp(-v)) * acc[g, 1, e]).astype(jnp.bfloat16)
            hit = lanes == expert * experts + e
            scale.append(jnp.sum(jnp.where(hit, route[g], 0.0), axis=1, keepdims=True))

    back = permutation(rows, True)

    def produce(j):
        for q in range(QUARTERS):
            down_in[j * QUARTERS + q].wait()
        for g in range(groups):
            parts = []
            for q in range(QUARTERS):
                span = slice(q * width + j * chunk, q * width + (j + 1) * chunk)
                total = None
                for e in range(experts):
                    part = scale[g * experts + e] * jnp.dot(
                        hid[g, e], down[e, :, span], preferred_element_type=jnp.float32
                    )
                    total = part if total is None else total + part
                parts.append(total.astype(jnp.bfloat16))
            tiled = jnp.dot(
                back, jnp.concatenate(parts, axis=0), preferred_element_type=jnp.float32
            )
            y_buf[j, g * GROUP : (g + 1) * GROUP] = tiled.astype(jnp.bfloat16).reshape(
                GROUP, TILE, chunk
            )
        push(
            y_buf.at[j, pl.ds(far * plane, plane)],
            r_core.at[j],
            rc_send.at[j],
            rc_recv.at[j],
            peer(z, far, y),
        )

    def pair(j, y_at):
        own = y_buf[j, pl.ds(block(c, y_at, 0), n_z)].astype(jnp.float32)
        return own + r_core[j, pl.ds(y_at * n_z, n_z)].astype(jnp.float32)

    def over_y(j):
        arrived(r_core.at[j], rc_send.at[j], rc_recv.at[j], peer(z, far, y))
        for step in range(1, n_y):
            s_buf[j, step - 1] = pair(j, y_next(step)).astype(jnp.bfloat16)
            push(
                s_buf.at[j, step - 1],
                r_y.at[j, step - 1],
                ry_send.at[j, step],
                ry_recv.at[j, step],
                peer(z, c, y_next(step)),
            )

    def over_z(j):
        total = pair(j, y)
        for step in range(1, n_y):
            arrived(
                r_y.at[j, step - 1],
                ry_send.at[j, step],
                ry_recv.at[j, step],
                peer(z, c, y_next(step)),
            )
            total = total + r_y[j, step - 1].astype(jnp.float32)
        t_buf[j] = total.astype(jnp.bfloat16)
        for step in range(n_z - 1, 0, -1):
            push(
                t_buf.at[j, z_next(step)],
                r_z.at[j, step - 1],
                rz_send.at[j, step],
                rz_recv.at[j, step],
                peer(z_next(step), c, y),
            )

    def finish(j):
        total = t_buf[j, z].astype(jnp.float32)
        for step in range(1, n_z):
            arrived(
                r_z.at[j, step - 1],
                rz_send.at[j, step],
                rz_recv.at[j, step],
                peer(z_next(step), c, y),
            )
            total = total + r_z[j, step - 1].astype(jnp.float32)
        final[...] = total
        for q in range(QUARTERS):
            span = slice(q * width + j * chunk, q * width + (j + 1) * chunk)
            out[:, span] = final[q * rows : (q + 1) * rows, :].astype(out.dtype)

    for t in range(CHUNKS + 3):
        for late, stage_of in enumerate((produce, over_y, over_z, finish)):
            if 0 <= t - late < CHUNKS:
                stage_of(t - late)
    for copy in sent:
        copy.wait_send()


def body(tokens, route_ids, route_weight, gate_weight, up_weight, down_weight):
    rows, features = tokens.shape
    n_z = lax.axis_size("expert") // CORES
    n_y = lax.axis_size("cuts")
    experts, _, units = gate_weight.shape
    width = features // QUARTERS
    chunk = width // CHUNKS
    plane = n_z * n_y
    blocks = CORES * plane
    groups = blocks // GROUP
    bf16, f32 = jnp.bfloat16, jnp.float32
    dma = pltpu.SemaphoreType.DMA
    vmem = pl.BlockSpec(memory_space=pltpu.VMEM)
    hbm = pl.BlockSpec(memory_space=pl.ANY)
    return pl.pallas_call(
        functools.partial(kernel, n_z, n_y),
        out_shape=jax.ShapeDtypeStruct((rows, features), bf16),
        in_specs=[vmem, vmem, vmem, hbm, hbm, hbm],
        out_specs=vmem,
        scratch_shapes=[
            pltpu.VMEM(gate_weight.shape, bf16),
            pltpu.VMEM(up_weight.shape, bf16),
            pltpu.VMEM(down_weight.shape, bf16),
            pltpu.VMEM((blocks, TILE, width + BLOCK), bf16),
            pltpu.VMEM((TILE, width + BLOCK), f32),
            pltpu.VMEM((groups, 2, experts, GROUP * rows, units), f32),
            pltpu.VMEM((groups, experts, GROUP * rows, units), bf16),
            pltpu.VMEM((groups, GROUP * TILE, width), bf16),
            pltpu.VMEM((CHUNKS, blocks, TILE, chunk), bf16),
            pltpu.VMEM((CHUNKS, plane, TILE, chunk), bf16),
            pltpu.VMEM((CHUNKS, n_y - 1, n_z, TILE, chunk), bf16),
            pltpu.VMEM((CHUNKS, n_y - 1, n_z, TILE, chunk), bf16),
            pltpu.VMEM((CHUNKS, n_z, TILE, chunk), bf16),
            pltpu.VMEM((CHUNKS, n_z - 1, TILE, chunk), bf16),
            pltpu.VMEM((TILE, chunk), f32),
            dma((QUARTERS,)),
            dma((QUARTERS,)),
            dma((CHUNKS * QUARTERS,)),
            dma((n_z,)),
            dma((n_z,)),
            dma((n_y, n_z)),
            dma((n_y, n_z)),
            dma((n_y, n_z)),
            dma((n_y, n_z)),
            dma((CHUNKS,)),
            dma((CHUNKS,)),
            dma((CHUNKS, n_y)),
            dma((CHUNKS, n_y)),
            dma((CHUNKS, n_z)),
            dma((CHUNKS, n_z)),
        ],
        compiler_params=pltpu.CompilerParams(
            collective_id=0, has_side_effects=True, vmem_limit_bytes=60 * 1024 * 1024
        ),
    )(tokens, route_ids, route_weight, gate_weight, up_weight, down_weight)


def solution(mesh):
    in_specs = (
        P(("parts", "expert", "cuts"), None),
        P(("parts", "expert", "cuts"), None),
        P(("parts", "expert", "cuts"), None),
        P("expert", None, "cuts"),
        P("expert", None, "cuts"),
        P("expert", "cuts", None),
    )
    out_specs = P(("parts", "expert", "cuts"), None)
    return jax.shard_map(body, mesh=mesh, in_specs=in_specs, out_specs=out_specs, check_vma=False)
```

time: 118 us -> 41.6 us (0.35)
  the two profiles are of different devices: /device:TPU:11 before, /device:TPU:0 now
where the time goes in v1:
time: 41.6 us; the launch traced here: 41.3 us
  Pallas kernels  39.9 us (96%)
  local copies, waits for them, and re-layouts  1.46 us (4%)
    pallas_call x1, Pallas kernels, body(): pl.pallas_call(functools.partial(kernel, n_z, n_y), out_shape=jax.ShapeDt...  39.9 us
    unnamed x1, local copies, waits for them, and re-layouts  1.46 us

profile of v1, /device:TPU:0, one launch (start us, length us, event | category | flops | bytes accessed | tf_op | source)
XLA Modules:
  0.0 41.3 jit_solution(400313224784319371)
XLA Ops:
  0.0 39.9 %shard_map.64 = bf16[4,7168]{1,0:T(4,128)(2,1)} custom-call(bf16[4,7168]{1,0:T(4,128)(2,1)} %tokens.1, s32[4,8]{1,0:T(4,128)} %ids.1, f32[4,8]{1,0:T(4,128)} %weights.1, bf16[2,7168,512]{2,1,0:T(8,128)(2,1)} %gate_hbm.1, bf16[2,7168,512]{2,1,0:T(8,128)(2,1)} %up_hbm.1, bf16[2,512,7168]{2,1,0:T(8,128)(2,1)} %down_hbm.1), custom_call_target="tpu_custom_call" | custom-call | tf_op jit(solution)/shard_map/pallas_call | solution.py:388
  39.9 1.5 %copy.8 = bf16[4,7168]{1,0:T(4,128)(2,1)} copy(bf16[4,7168]{1,0:T(4,128)(2,1)} %shard_map.64) | data formatting | bytes 114688

commit v2 on v1

--- a/solution.py
+++ b/solution.py
@@ -15,7 +15,8 @@
 QUARTERS = 4
 TILE = 16
 GROUP = 16
-CHUNKS = 2
+CHUNKS = 7
+LAG = 3
 MESH = pl.DeviceIdType.MESH
 
 
@@ -91,6 +92,8 @@
     y = lax.axis_index("cuts")
     z, c = expert // CORES, expert % CORES
     far = 1 - c
+    cut = (width // 256 + 1) // 2 * 256
+    spans = ((0, cut), (cut, width + BLOCK))
 
     def peer(z_at, c_at, y_at):
         return {"expert": z_at * CORES + c_at, "cuts": y_at}
@@ -111,23 +114,22 @@
         return lax.rem(y + n_y - step, n_y)
 
     gate_in, up_in, down_in = [], [], []
-    for q in range(QUARTERS):
-        span = pl.ds(q * width, width)
-        gate_in.append(
-            pltpu.make_async_copy(gate_hbm.at[:, span, :], gate.at[:, span, :], g_sem.at[q])
-        )
-        up_in.append(pltpu.make_async_copy(up_hbm.at[:, span, :], up.at[:, span, :], u_sem.at[q]))
-        gate_in[q].start()
-        up_in[q].start()
-    for j in range(CHUNKS):
+    for h in range(2):
+        low, high = spans[h][0], min(spans[h][1], width)
         for q in range(QUARTERS):
-            span = pl.ds(q * width + j * chunk, chunk)
-            down_in.append(
-                pltpu.make_async_copy(
-                    down_hbm.at[:, :, span], down.at[:, :, span], d_sem.at[j * QUARTERS + q]
-                )
-            )
-            down_in[-1].start()
+            span = pl.ds(q * width + low, high - low)
+            at = h * QUARTERS + q
+            gate_in.append(
+                pltpu.make_async_copy(gate_hbm.at[:, span, :], gate.at[:, span, :], g_sem.at[at])
+            )
+            up_in.append(
+                pltpu.make_async_copy(up_hbm.at[:, span, :], up.at[:, span, :], u_sem.at[at])
+            )
+            gate_in[at].start()
+            up_in[at].start()
+    for e in range(experts):
+        down_in.append(pltpu.make_async_copy(down_hbm.at[e], down.at[e], d_sem.at[e]))
+        down_in[e].start()
 
     barrier = pltpu.get_barrier_semaphore()
     for step in range(1, n_z):
@@ -194,85 +196,117 @@
             device_id_type=MESH,
         ).wait_recv()
 
-    def to_y(z_step, slot):
+    def half(h, slot):
+        return gathered.at[slot, :, pl.ds(spans[h][0], spans[h][1] - spans[h][0])]
+
+    def to_y(h, z_step, slot):
         for step in range(1, n_y):
             push(
-                gathered.at[slot],
-                gathered.at[slot],
-                ay_send.at[step, z_step],
-                ay_recv.at[step, z_step],
+                half(h, slot),
+                half(h, slot),
+                ay_send.at[h, step, z_step],
+                ay_recv.at[h, step, z_step],
                 peer(z, c, y_next(step)),
             )
 
-    def to_core(y_step, z_step, slot):
+    def to_core(h, y_step, z_step, slot):
         push(
-            gathered.at[slot],
-            gathered.at[slot],
-            ac_send.at[y_step, z_step],
-            ac_recv.at[y_step, z_step],
+            half(h, slot),
+            half(h, slot),
+            ac_send.at[h, y_step, z_step],
+            ac_recv.at[h, y_step, z_step],
             peer(z, far, y),
         )
 
-    for step in range(n_z - 1, 0, -1):
-        push(
-            gathered.at[mine],
-            gathered.at[mine],
-            az_send.at[step],
-            az_recv.at[step],
-            peer(z_next(step), c, y),
-        )
-    to_y(0, mine)
-    to_core(0, 0, mine)
-    for z_step in range(1, n_z):
+    def begin(h):
+        for step in range(1, n_z):
+            push(
+                half(h, mine),
+                half(h, mine),
+                az_send.at[h, step],
+                az_recv.at[h, step],
+                peer(z_next(step), c, y),
+            )
+        to_y(h, 0, mine)
+        to_core(h, 0, 0, mine)
+
+    def from_z(h, z_step):
         slot = block(c, y, z_prev(z_step))
         arrived(
-            gathered.at[slot], az_send.at[z_step], az_recv.at[z_step], peer(z_next(z_step), c, y)
-        )
-        to_y(z_step, slot)
-        to_core(0, z_step, slot)
-    for z_step in range(n_z):
-        for y_step in range(1, n_y):
-            slot = block(c, y_prev(y_step), z_prev(z_step))
-            arrived(
-                gathered.at[slot],
-                ay_send.at[y_step, z_step],
-                ay_recv.at[y_step, z_step],
-                peer(z, c, y_next(y_step)),
-            )
-            to_core(y_step, z_step, slot)
-    for z_step in range(n_z):
-        for y_step in range(n_y):
-            slot = block(far, y_prev(y_step), z_prev(z_step))
-            arrived(
-                gathered.at[slot],
-                ac_send.at[y_step, z_step],
-                ac_recv.at[y_step, z_step],
-                peer(z, far, y),
-            )
+            half(h, slot),
+            az_send.at[h, z_step],
+            az_recv.at[h, z_step],
+            peer(z_next(z_step), c, y),
+        )
+        to_y(h, z_step, slot)
+        to_core(h, 0, z_step, slot)
+
+    def from_y(h, z_step, y_step):
+        slot = block(c, y_prev(y_step), z_prev(z_step))
+        arrived(
+            half(h, slot),
+            ay_send.at[h, y_step, z_step],
+            ay_recv.at[h, y_step, z_step],
+            peer(z, c, y_next(y_step)),
+        )
+        to_core(h, y_step, z_step, slot)
+
+    def events(h):
+        steps = [functools.partial(from_z, h, z_step) for z_step in range(1, n_z)]
+        return steps + [
+            functools.partial(from_y, h, z_step, y_step)
+            for z_step in range(n_z)
+            for y_step in range(1, n_y)
+        ]
+
+    def from_core(h):
+        for z_step in range(n_z):
+            for y_step in range(n_y):
+                slot = block(far, y_prev(y_step), z_prev(z_step))
+                arrived(
+                    half(h, slot),
+                    ac_send.at[h, y_step, z_step],
+                    ac_recv.at[h, y_step, z_step],
+                    peer(z, far, y),
+                )
+
+    begin(0)
+    begin(1)
+    first, second = events(0), events(1)
+    for event in first[: n_z - 1] + second[: n_z - 1] + first[n_z - 1 :]:
+        event()
+    pending = second[n_z - 1 :]
+    each = -(-len(pending) // (2 * QUARTERS))
 
     order = permutation(rows, False)
     per = GROUP * rows
     route = []
-    for g in range(groups):
-        flat = gathered[g * GROUP : (g + 1) * GROUP].reshape(GROUP * TILE, width + BLOCK)
-        ordered = jnp.dot(order, flat, preferred_element_type=jnp.float32)
-        wide[g] = ordered[:, :width].astype(jnp.bfloat16)
-        terms = ordered[:, width:]
-        route.append(terms[:per] + terms[per : 2 * per] + terms[2 * per : 3 * per])
-    for q in range(QUARTERS):
-        span = slice(q * width, (q + 1) * width)
-        gate_in[q].wait()
+    for h in range(2):
+        for event in pending if h else []:
+            event()
+        from_core(h)
+        low, high = spans[h][0], min(spans[h][1], width)
         for g in range(groups):
-            x = wide[g, q * per : (q + 1) * per, :]
-            for e in range(experts):
-                part = jnp.dot(x, gate[e, span, :], preferred_element_type=jnp.float32)
-                acc[g, 0, e] = part if q == 0 else acc[g, 0, e] + part
-        up_in[q].wait()
-        for g in range(groups):
-            x = wide[g, q * per : (q + 1) * per, :]
-            for e in range(experts):
-                part = jnp.dot(x, up[e, span, :], preferred_element_type=jnp.float32)
-                acc[g, 1, e] = part if q == 0 else acc[g, 1, e] + part
+            flat = gathered[g * GROUP : (g + 1) * GROUP, :, low : spans[h][1]]
+            flat = flat.reshape(GROUP * TILE, spans[h][1] - low)
+            ordered = jnp.dot(order, flat, preferred_element_type=jnp.float32)
+            wide[g, :, low:high] = ordered[:, : high - low].astype(jnp.bfloat16)
+            if h:
+                terms = ordered[:, high - low :]
+                route.append(terms[:per] + terms[per : 2 * per] + terms[2 * per : 3 * per])
+        for q in range(QUARTERS):
+            span = slice(q * width + low, q * width + high)
+            for side, (held, coming) in enumerate(((gate, gate_in), (up, up_in))):
+                coming[h * QUARTERS + q].wait()
+                for g in range(groups):
+                    x = wide[g, q * per : (q + 1) * per, low:high]
+                    for e in range(experts):
+                        part = jnp.dot(x, held[e, span, :], preferred_element_type=jnp.float32)
+                        acc[g, side, e] = part if h + q == 0 else acc[g, side, e] + part
+                if h == 0:
+                    for event in pending[:each]:
+                        event()
+                    pending = pending[each:]
     lanes = lax.broadcasted_iota(jnp.int32, (per, BLOCK), 1)
     scale = []
     for g in range(groups):
@@ -283,10 +317,10 @@
             scale.append(jnp.sum(jnp.where(hit, route[g], 0.0), axis=1, keepdims=True))
 
     back = permutation(rows, True)
+    for e in range(experts):
+        down_in[e].wait()
 
     def produce(j):
-        for q in range(QUARTERS):
-            down_in[j * QUARTERS + q].wait()
         for g in range(groups):
             parts = []
             for q in range(QUARTERS):
@@ -363,10 +397,10 @@
             span = slice(q * width + j * chunk, q * width + (j + 1) * chunk)
             out[:, span] = final[q * rows : (q + 1) * rows, :].astype(out.dtype)
 
-    for t in range(CHUNKS + 3):
+    for t in range(CHUNKS + 3 * LAG):
         for late, stage_of in enumerate((produce, over_y, over_z, finish)):
-            if 0 <= t - late < CHUNKS:
-                stage_of(t - late)
+            if 0 <= t - late * LAG < CHUNKS:
+                stage_of(t - late * LAG)
     for copy in sent:
         copy.wait_send()
 
@@ -406,15 +440,15 @@
             pltpu.VMEM((CHUNKS, n_z, TILE, chunk), bf16),
             pltpu.VMEM((CHUNKS, n_z - 1, TILE, chunk), bf16),
             pltpu.VMEM((TILE, chunk), f32),
-            dma((QUARTERS,)),
-            dma((QUARTERS,)),
-            dma((CHUNKS * QUARTERS,)),
-            dma((n_z,)),
-            dma((n_z,)),
-            dma((n_y, n_z)),
-            dma((n_y, n_z)),
-            dma((n_y, n_z)),
-            dma((n_y, n_z)),
+            dma((2 * QUARTERS,)),
+            dma((2 * QUARTERS,)),
+            dma(down_weight.shape[:1]),
+            dma((2, n_z)),
+            dma((2, n_z)),
+            dma((2, n_y, n_z)),
+            dma((2, n_y, n_z)),
+            dma((2, n_y, n_z)),
+            dma((2, n_y, n_z)),
             dma((CHUNKS,)),
             dma((CHUNKS,)),
             dma((CHUNKS, n_y)),
@@ -423,7 +457,7 @@
             dma((CHUNKS, n_z)),
         ],
         compiler_params=pltpu.CompilerParams(
-            collective_id=0, has_side_effects=True, vmem_limit_bytes=60 * 1024 * 1024
+            collective_id=0, has_side_effects=True, vmem_limit_bytes=52 * 1024 * 1024
         ),
     )(tokens, route_ids, route_weight, gate_weight, up_weight, down_weight)
 

time: 41.6 us -> 39.6 us (0.952)
  Pallas kernels: 39.9 us -> 36.6 us
  local copies, waits for them, and re-layouts: 1.46 us -> 2.81 us
    pallas_call x1, Pallas kernels: 39.9 us -> 36.6 us  [body(): pl.pallas_call(functools.partial(kernel, n_z, n_y), out_shape=jax.ShapeDt...]
    unnamed x1 -> x7, local copies, waits for them, and re-layouts: 1.46 us -> 2.81 us
where the time goes in v2:
time: 39.6 us; the launch traced here: 39.4 us
  Pallas kernels  36.6 us (92%)
  local copies, waits for them, and re-layouts  2.81 us (7%)
    pallas_call x1, Pallas kernels, body(): pl.pallas_call(functools.partial(kernel, n_z, n_y), out_shape=jax.ShapeDt...  36.6 us
    unnamed x7, local copies, waits for them, and re-layouts  2.81 us

profile of v2, /device:TPU:0, one launch (start us, length us, event | category | flops | bytes accessed | tf_op | source)
XLA Modules:
  0.0 39.4 jit_solution(11239305534280830843)
XLA Ops:
  0.0 0.0 copy-start
  0.0 0.8 %copy-done = bf16[4,7168]{1,0:T(4,128)(2,1)S(1)} copy-done((bf16[4,7168]{1,0:T(4,128)(2,1)S(1)}, bf16[4,7168]{1,0:T(4,128)(2,1)}, u32[]{:S(2)}) %copy-start) | copy-done | bytes 57368
  0.8 0.0 copy-start.1
  0.8 0.7 %copy-done.1 = s32[4,8]{1,0:T(4,128)S(1)} copy-done((s32[4,8]{1,0:T(4,128)S(1)}, s32[4,8]{1,0:T(4,128)}, u32[]{:S(2)}) %copy-start.1) | copy-done | bytes 152
  1.5 0.0 copy-start.2
  1.5 0.7 %copy-done.2 = f32[4,8]{1,0:T(4,128)S(1)} copy-done((f32[4,8]{1,0:T(4,128)S(1)}, f32[4,8]{1,0:T(4,128)}, u32[]{:S(2)}) %copy-start.2) | copy-done | bytes 152
  2.2 36.6 %shard_map.64 = bf16[4,7168]{1,0:T(4,128)(2,1)S(1)} custom-call(bf16[4,7168]{1,0:T(4,128)(2,1)S(1)} %copy-done, s32[4,8]{1,0:T(4,128)S(1)} %copy-done.1, f32[4,8]{1,0:T(4,128)S(1)} %copy-done.2, bf16[2,7168,512]{2,1,0:T(8,128)(2,1)} %gate_hbm.1, bf16[2,7168,512]{2,1,0:T(8,128)(2,1)} %up_hbm.1, bf16[2,512,7168]{2,1,0:T(8,128)(2,1)} %down_hbm.1), custom_call_target="tpu_custom_call" | custom-call | tf_op jit(solution)/shard_map/pallas_call | solution.py:422
  38.8 0.6 %copy.8 = bf16[4,7168]{1,0:T(4,128)(2,1)} copy(bf16[4,7168]{1,0:T(4,128)(2,1)S(1)} %shard_map.64) | data formatting | bytes 114688
Async XLA Ops:
  0.0 0.8 %copy-start = (bf16[4,7168]{1,0:T(4,128)(2,1)S(1)}, bf16[4,7168]{1,0:T(4,128)(2,1)}, u32[]{:S(2)}) copy-start(bf16[4,7168]{1,0:T(4,128)(2,1)} %tokens.1) | copy-start | bytes 172036
  0.8 0.7 %copy-start.1 = (s32[4,8]{1,0:T(4,128)S(1)}, s32[4,8]{1,0:T(4,128)}, u32[]{:S(2)}) copy-start(s32[4,8]{1,0:T(4,128)} %ids.1) | copy-start | bytes 388
  1.5 0.7 %copy-start.2 = (f32[4,8]{1,0:T(4,128)S(1)}, f32[4,8]{1,0:T(4,128)}, u32[]{:S(2)}) copy-start(f32[4,8]{1,0:T(4,128)} %weights.1) | copy-start | bytes 388

commit v3 on v2

--- a/solution.py
+++ b/solution.py
@@ -398,7 +398,7 @@
             out[:, span] = final[q * rows : (q + 1) * rows, :].astype(out.dtype)
 
     for t in range(CHUNKS + 3 * LAG):
-        for late, stage_of in enumerate((produce, over_y, over_z, finish)):
+        for late, stage_of in reversed(tuple(enumerate((produce, over_y, over_z, finish)))):
             if 0 <= t - late * LAG < CHUNKS:
                 stage_of(t - late * LAG)
     for copy in sent:

time: 39.6 us -> 41.9 us (1.058)
  Pallas kernels: 36.6 us -> 38.9 us
    pallas_call x1, Pallas kernels: 36.6 us -> 38.9 us  [body(): pl.pallas_call(functools.partial(kernel, n_z, n_y), out_shape=jax.ShapeDt...]
where the time goes in v3:
time: 41.9 us; the launch traced here: 41.7 us
  Pallas kernels  38.9 us (93%)
  local copies, waits for them, and re-layouts  2.81 us (7%)
    pallas_call x1, Pallas kernels, body(): pl.pallas_call(functools.partial(kernel, n_z, n_y), out_shape=jax.ShapeDt...  38.9 us
    unnamed x7, local copies, waits for them, and re-layouts  2.81 us

profile of v3, /device:TPU:0, one launch (start us, length us, event | category | flops | bytes accessed | tf_op | source)
XLA Modules:
  0.0 41.7 jit_solution(13336357368960954126)
XLA Ops:
  0.0 0.0 copy-start
  0.0 0.8 %copy-done = bf16[4,7168]{1,0:T(4,128)(2,1)S(1)} copy-done((bf16[4,7168]{1,0:T(4,128)(2,1)S(1)}, bf16[4,7168]{1,0:T(4,128)(2,1)}, u32[]{:S(2)}) %copy-start) | copy-done | bytes 57368
  0.8 0.0 copy-start.1
  0.8 0.7 %copy-done.1 = s32[4,8]{1,0:T(4,128)S(1)} copy-done((s32[4,8]{1,0:T(4,128)S(1)}, s32[4,8]{1,0:T(4,128)}, u32[]{:S(2)}) %copy-start.1) | copy-done | bytes 152
  1.5 0.0 copy-start.2
  1.5 0.7 %copy-done.2 = f32[4,8]{1,0:T(4,128)S(1)} copy-done((f32[4,8]{1,0:T(4,128)S(1)}, f32[4,8]{1,0:T(4,128)}, u32[]{:S(2)}) %copy-start.2) | copy-done | bytes 152
  2.2 38.9 %shard_map.64 = bf16[4,7168]{1,0:T(4,128)(2,1)S(1)} custom-call(bf16[4,7168]{1,0:T(4,128)(2,1)S(1)} %copy-done, s32[4,8]{1,0:T(4,128)S(1)} %copy-done.1, f32[4,8]{1,0:T(4,128)S(1)} %copy-done.2, bf16[2,7168,512]{2,1,0:T(8,128)(2,1)} %gate_hbm.1, bf16[2,7168,512]{2,1,0:T(8,128)(2,1)} %up_hbm.1, bf16[2,512,7168]{2,1,0:T(8,128)(2,1)} %down_hbm.1), custom_call_target="tpu_custom_call" | custom-call | tf_op jit(solution)/shard_map/pallas_call | solution.py:422
  41.1 0.6 %copy.8 = bf16[4,7168]{1,0:T(4,128)(2,1)} copy(bf16[4,7168]{1,0:T(4,128)(2,1)S(1)} %shard_map.64) | data formatting | bytes 114688
Async XLA Ops:
  0.0 0.8 %copy-start = (bf16[4,7168]{1,0:T(4,128)(2,1)S(1)}, bf16[4,7168]{1,0:T(4,128)(2,1)}, u32[]{:S(2)}) copy-start(bf16[4,7168]{1,0:T(4,128)(2,1)} %tokens.1) | copy-start | bytes 172036
  0.8 0.7 %copy-start.1 = (s32[4,8]{1,0:T(4,128)S(1)}, s32[4,8]{1,0:T(4,128)}, u32[]{:S(2)}) copy-start(s32[4,8]{1,0:T(4,128)} %ids.1) | copy-start | bytes 388
  1.5 0.7 %copy-start.2 = (f32[4,8]{1,0:T(4,128)S(1)}, f32[4,8]{1,0:T(4,128)}, u32[]{:S(2)}) copy-start(f32[4,8]{1,0:T(4,128)} %weights.1) | copy-start | bytes 388
